TPU v7x, 256 devices: a whole 4x4x8 slice. The times are simulated.
256 devices in a mesh: tm: 4 (over z_lo, core), band: 64 (over y, z_hi, x).
Axes of the slice: x: 4, y: 4, z: 8 (z_hi: 4, z_lo: 2; z = z_hi * 2 + z_lo), core: 2. Of those that a mesh axis runs over, the one named last changes fastest.
Arguments:
- volts: bfloat16 [2, 1024, 262144], P(None, 'band', 'tm'), may hold values from -4 to 4
- taps: float32 [8, 256], replicated, may hold values from -2 to 2
Outputs:
- visibilities: float32 [256, 2, 1024, 1024], P(('tm', 'band'))
All inputs are finite; a program needn't handle non-finite values.
Results may differ from a plain program's by a relative error of at most 0.0046.
Values may be sent and summed in bfloat16 or wider, within the bound.
No kernel may reach another device: no remote copies, remote signals or barrier semaphores. Data moves between devices by JAX's collectives and lax.ppermute only.
A program may use at most 128 MiB of HBM per device.

v0:
```python
import math

import jax
import jax.numpy as jnp
from jax import lax
from jax.sharding import PartitionSpec as P


def shifted(shard, axis, by):
    size = lax.axis_size(axis)
    pairs = [(i, i + by) for i in range(size) if 0 <= i + by < size]
    return lax.ppermute(shard, axis, pairs)


def dft_table(channels):
    index = jnp.arange(channels, dtype=jnp.int32)
    turns = index[:, None] * index[None, :] % channels
    theta = turns.astype(jnp.float32) * (2.0 * math.pi / channels)
    factor = 1.0 / math.sqrt(channels)
    cosine = jnp.cos(theta) * factor
    sine = jnp.sin(theta) * factor
    real_row = jnp.stack([cosine, sine], axis=1)
    imag_row = jnp.stack([-sine, cosine], axis=1)
    table = jnp.stack([real_row, imag_row], axis=1)
    return table.reshape(2 * channels, 2, channels).astype(jnp.bfloat16)


def weighting(signal):
    swapped = jnp.stack([signal[:, 1], -signal[:, 0]], axis=1)
    return jnp.stack([signal, swapped], axis=1)


def square_products(signal):
    return jnp.einsum(
        "corps,crqs->copq", weighting(signal), signal, preferred_element_type=jnp.float32
    )


def correlate(signal):
    return square_products(signal)


def per_device(volts, taps):
    time_groups = lax.axis_size("tm")
    band_groups = lax.axis_size("band")
    taps_count = taps.shape[0]
    channels = taps.shape[1]
    local_inputs = volts.shape[1]
    samples = volts.shape[2]
    spec_local = samples // channels
    own_channels = channels // (time_groups * band_groups)
    margin = (taps_count - 1) * channels
    history = shifted(volts[:, :, samples - margin :], "tm", 1)
    frames = jnp.concatenate([history, volts], axis=2)
    frames = frames.reshape(2, local_inputs, spec_local + taps_count - 1, channels).astype(
        jnp.float32
    )
    filtered = taps[0] * frames[:, :, 0:spec_local, :]
    for weight_index in range(1, taps_count):
        filtered = (
            filtered
            + taps[weight_index] * frames[:, :, weight_index : weight_index + spec_local, :]
        )
    filtered = filtered.astype(jnp.bfloat16)
    table = dft_table(channels)
    spectra = lax.dot_general(
        table, filtered, (((1, 2), (0, 3)), ((), ())), preferred_element_type=jnp.float32
    )
    spectra = spectra.astype(jnp.bfloat16).reshape(
        time_groups, band_groups, own_channels, 2, local_inputs, spec_local
    )
    spectra_total = spec_local * time_groups
    turned = lax.all_to_all(
        lax.all_to_all(spectra, "tm", split_axis=0, concat_axis=5, tiled=True),
        "band",
        split_axis=1,
        concat_axis=4,
        tiled=True,
    )
    result = correlate(turned.reshape(own_channels, 2, turned.shape[4], spectra_total))
    return result * (1.0 / spectra_total)


def solution(mesh):
    in_specs = (P(None, "band", "tm"), P())
    out_specs = P(("tm", "band"), None, None, None)
    return jax.shard_map(
        per_device, mesh=mesh, in_specs=in_specs, out_specs=out_specs, check_vma=False
    )
```

profile of v0, /device:TPU:6, one launch (start us, length us, event | category | flops | bytes accessed | tf_op | source)
XLA Modules:
  0.0 222.8 jit_solution(3602252751473017862)
XLA Ops:
  0.0 0.9 slice.58
  0.9 1.7 collective-permute-start
  2.6 1.0 fusion.23
  3.6 1.1 negate_convert_fusion
  4.8 0.1 pad_maximum_fusion
  4.9 0.5 copy.18
  5.4 0.2 reshape.119
  5.6 1.0 fusion.26
  6.6 0.0 collective-permute-done
  6.6 6.1 %maximum_convert_fusion = f32[2,16,67328]{2,1,0:T(8,128)} fusion(bf16[2,16,65536]{2,1,0:T(8,128)(2,1)} %param.2, bf16[2,16,1792]{2,1,0:T(8,128)(2,1)S(1)} %collective-permute-done), kind=kLoop, calls=%fused_computation.23 | loop fusion | flops 8617984 | bytes 12926976 | tf_op jit(solution)/shard_map/convert_element_type | solution.py:55
  12.7 7.5 %reshape.118 = f32[2,16,263,256]{3,2,1,0:T(8,128)} reshape(f32[2,16,67328]{2,1,0:T(8,128)} %maximum_convert_fusion) | data formatting | bytes 17235968 | tf_op jit(solution)/shard_map/convert_element_type | solution.py:55
  20.2 27.0 %bitcast_convert_fusion = bf16[512,16,256]{2,0,1:T(8,128)(2,1)S(1)} fusion(f32[2,16,263,256]{3,2,1,0:T(8,128)} %reshape.118, f32[256]{0:T(256)S(1)} %bitcast.66, f32[256]{0:T(256)S(1)} %bitcast.67, f32[256]{0:T(256)S(1)} %bitcast.61, f32[256]{0:T(256)S(1)} %bitcast.62, f32[256]{0:T(256)S(1)} %bitcast.63, f32[256]{0:T(256)S(1)} %bitcast.64, ...), kind=kOutput, calls=%fused_computation.16 | convolution fusion | flops 2183135232 | bytes 71835648 | tf_op jit(solution)/shard_map/dot_general | solution.py:66
  47.2 2.4 %copy.28 = bf16[512,16,256]{2,1,0:T(8,128)(2,1)S(1)} copy(bf16[512,16,256]{2,0,1:T(8,128)(2,1)S(1)} %bitcast_convert_fusion) | data formatting | bytes 8388608 | tf_op jit(solution)/shard_map/reshape | solution.py:69
  49.6 51.5 %all_to_all.33 = bf16[4,64,1,2,16,256]{5,4,3,1,2,0:T(8,128)(2,1)S(1)} all-to-all(bf16[4,64,1,2,16,256]{5,4,3,1,2,0:T(8,128)(2,1)S(1)} %bitcast.56), channel_id=1, replica_groups=mesh['tm'=4,'band'=64] {'tm'}, dimensions={0} | all-to-all | bytes 8388608 | tf_op jit(solution)/shard_map/all_to_all | solution.py:74
  101.1 0.6 copy.29
  101.7 108.5 %all_to_all.34 = bf16[1,64,1,2,16,1024]{5,4,3,2,0,1:T(8,128)(2,1)S(1)} all-to-all(bf16[1,64,1,2,16,1024]{5,4,3,2,0,1:T(8,128)(2,1)S(1)} %bitcast.58), channel_id=1, replica_groups=mesh['tm'=4,'band'=64] {'band'}, dimensions={1} | all-to-all | bytes 8388608 | tf_op jit(solution)/shard_map/all_to_all | solution.py:73
  210.1 0.5 copy.23
  210.7 0.3 fusion.25
  211.0 0.4 maximum_bitcast_fusion.2
  211.4 11.4 %fusion.11 = f32[1,2,1024,1024]{3,2,1,0:T(8,128)} fusion(bf16[2,1024,1024,1]{2,1,0,3:T(8,128)(2,1)S(1)} %bitcast.54, bf16[1,1,2,1024,1024]{4,3,2,1,0:T(8,128)(2,1)S(1)} %maximum_bitcast_fusion.2, bf16[1,1,2,1024,1024]{4,3,2,1,0:T(8,128)(2,1)S(1)} %bitcast.55), kind=kOutput, calls=%fused_computation.22 | convolution fusion | flops 8596226048 | bytes 20971520 | tf_op jit(solution)/shard_map/corps,crqs->copq/dot_general | solution.py:34
  (1 shorter events, 0.0 us)
Async XLA Ops:
  0.9 5.7 %collective-permute-start = (bf16[2,16,1792]{2,1,0:T(8,128)(2,1)S(1)}, bf16[2,16,1792]{2,1,0:T(8,128)(2,1)S(1)}, u32[]{:S(2)}, u32[]{:S(2)}) collective-permute-start(bf16[2,16,1792]{2,1,0:T(8,128)(2,1)S(1)} %slice.58), channel_id=1, source_target_pairs={{0,64},{64,128},{128,192},{1,65},{65,129},{129,193},{2,66},{66,130... | collective-permute-start | bytes 344072 | tf_op jit(solution)/shard_map/ppermute | solution.py:12
where the time goes:
time: 226 us; the launch traced here: 223 us
  blocking collectives  160 us (71%)
  matrix products  38.4 us (17%)
  local copies, waits for them, and re-layouts  13.7 us (6%)
  other arithmetic  8.91 us (4%)
    all_to_all x1, blocking collectives, per_device(): lax.all_to_all(lax.all_to_all(spectra, 'tm', split_axis=0, concat_axis=5,...  108 us
    all_to_all x1, blocking collectives, per_device(): lax.all_to_all(spectra, 'tm', split_axis=0, concat_axis=5, tiled=True)  51.5 us
    dot_general x1, matrix products, per_device(): lax.dot_general(table, filtered, (((1, 2), (0, 3)), ((), ())), preferred_...  27 us
    dot_general x1, matrix products, square_products(): jnp.einsum('corps,crqs->copq', weighting(signal), signal, preferred_eleme...  11.4 us
    convert_element_type x1, local copies, waits for them, and re-layouts, per_device(): frames.reshape(2, local_inputs, spec_local + taps_count - 1, channels)  7.52 us
    convert_element_type x1, other arithmetic, per_device(): frames.reshape(2, local_inputs, spec_local + taps_count - 1, channels)  6.06 us
  transfers between devices with their start and end apart: 1, of which 0 were waited for; matrix products, arithmetic and copies ran while one was open for 2% of the time, Pallas kernels for 0%

commit v1 on v0

v1 whole, which is shorter than its diff:
```python
import functools
import math

import jax
import jax.numpy as jnp
import ml_dtypes
import numpy as np
from jax import lax
from jax.experimental import pallas as pl
from jax.experimental.pallas import tpu as pltpu
from jax.sharding import PartitionSpec as P

LANES = 128
VMEM_BYTES = 56 * 1024 * 1024


def shifted(shard, axis, by):
    size = lax.axis_size(axis)
    pairs = [(i, i + by) for i in range(size) if 0 <= i + by < size]
    return lax.ppermute(shard, axis, pairs)


def dft_table(channels):
    index = np.arange(channels)
    theta = (index[:, None] * index[None, :] % channels) * (2.0 * math.pi / channels)
    factor = 1.0 / math.sqrt(channels)
    cosine = np.cos(theta) * factor
    sine = np.sin(theta) * factor
    real_row = np.stack([cosine, sine], axis=1)
    imag_row = np.stack([-sine, cosine], axis=1)
    table = np.stack([real_row, imag_row], axis=1)
    return table.reshape(2 * channels, 2 * channels).astype(np.float32).astype(ml_dtypes.bfloat16)


def channelize_kernel(volts_ref, history_ref, taps_ref, table_ref, out_ref, tail, rows, turned):
    taps_count, channels = taps_ref.shape
    inputs = volts_ref.shape[1]
    block = volts_ref.shape[2] // channels
    margin = taps_count - 1

    @pl.when(pl.program_id(0) == 0)
    def _():
        tail[...] = history_ref[...]

    for part in range(2):
        for left in range(0, channels, LANES):
            weights = [taps_ref[j : j + 1, left : left + LANES] for j in range(taps_count)]

            def frame(index):
                if index < margin:
                    at = index * channels + left
                    return tail[part, :, at : at + LANES].astype(jnp.float32)
                at = (index - margin) * channels + left
                return volts_ref[part, :, at : at + LANES].astype(jnp.float32)

            window = [frame(index) for index in range(margin)]
            for t in range(block):
                window.append(frame(t + margin))
                terms = [weights[j] * window[j] for j in range(taps_count)]
                while len(terms) > 1:
                    terms = [terms[n] + terms[n + 1] for n in range(0, len(terms), 2)]
                rows[(part * channels + left) // LANES, pl.ds(t, inputs, stride=block), :] = terms[0]
                window = window[1:]
    tail[...] = volts_ref[:, :, (block - margin) * channels :]

    together = 2
    bins = table_ref.shape[0]

    def one(step, carry):
        first = pl.multiple_of(step * together * block, together * block)
        signal = jnp.concatenate(
            [rows[n, pl.ds(first, together * block), :].astype(jnp.bfloat16) for n in range(rows.shape[0])], axis=1
        )
        found = lax.dot_general(
            table_ref[...], signal, (((1,), (1,)), ((), ())), preferred_element_type=jnp.float32
        )
        for n in range(together):
            turned[pl.ds(step * together + n, bins, stride=inputs), :] = found[:, n * block : (n + 1) * block]
        return carry

    lax.fori_loop(0, inputs // together, one, 0)
    out_ref[...] = turned[...].astype(jnp.bfloat16).reshape(out_ref.shape)


def channelize(volts, history, taps, block):
    taps_count, channels = taps.shape
    _, inputs, samples = volts.shape
    spectra = samples // channels
    return pl.pallas_call(
        channelize_kernel,
        grid=(spectra // block,),
        in_specs=[
            pl.BlockSpec((2, inputs, block * channels), lambda n: (0, 0, n)),
            pl.BlockSpec(history.shape, lambda n: (0, 0, 0)),
            pl.BlockSpec(taps.shape, lambda n: (0, 0)),
            pl.BlockSpec((2 * channels, 2 * channels), lambda n: (0, 0)),
        ],
        out_specs=pl.BlockSpec((channels, 2, inputs, block), lambda n: (0, 0, 0, n)),
        out_shape=jax.ShapeDtypeStruct((channels, 2, inputs, spectra), jnp.bfloat16),
        scratch_shapes=[
            pltpu.VMEM(history.shape, jnp.bfloat16),
            pltpu.VMEM((2 * channels // LANES, inputs * block, LANES), jnp.float32),
            pltpu.VMEM((2 * channels * inputs, block), jnp.float32),
        ],
        compiler_params=pltpu.CompilerParams(vmem_limit_bytes=VMEM_BYTES),
        cost_estimate=pl.CostEstimate(
            flops=2 * spectra * inputs * (4 * channels * channels + 2 * taps_count * channels),
            bytes_accessed=16 * spectra * inputs * channels,
            transcendentals=0,
        ),
    )(volts, history, taps, jnp.asarray(dft_table(channels)))


def correlate_kernel(scale, tile, signal_ref, out_ref, store, sems):
    groups, bands, _, inputs, _ = signal_ref.shape
    total = bands * inputs
    width = tile // inputs

    def side(at, plane, sign=1):
        picked = [
            signal_ref[g, at * width : (at + 1) * width, plane].reshape(tile, -1) for g in range(groups)
        ]
        return [-x if sign < 0 else x for x in picked]

    def copy(n, p, q):
        place = out_ref.at[0, :, pl.ds(p * tile, tile), pl.ds(q * tile, tile)]
        return pltpu.make_async_copy(store.at[:, pl.ds(p * tile, tile), pl.ds(q * tile, tile)], place, sems.at[n])

    copies = []

    def put(p, q, real, imag):
        where = (pl.ds(p * tile, tile), pl.ds(q * tile, tile))
        store[0, where[0], where[1]] = real
        store[1, where[0], where[1]] = imag
        started = copy(len(copies), p, q)
        started.start()
        copies.append(started)

    contract = (((1,), (1,)), ((), ()))
    for p in range(total // tile):
        left = jnp.concatenate(side(p, 0) + side(p, 1), axis=1)
        crossed = jnp.concatenate(side(p, 1) + side(p, 0, -1), axis=1)
        for q in range(p + 1):
            right = jnp.concatenate(side(q, 0) + side(q, 1), axis=1)
            real = lax.dot_general(left, right, contract, preferred_element_type=jnp.float32) * scale
            imag = lax.dot_general(crossed, right, contract, preferred_element_type=jnp.float32) * scale
            put(p, q, real, imag)
            if p != q:
                put(q, p, real.T, -imag.T)
    for started in copies:
        started.wait()


def correlate(signal):
    groups, bands, _, inputs, spectra = signal.shape
    total = bands * inputs
    tile = 256
    blocks = (total // tile) ** 2
    return pl.pallas_call(
        functools.partial(correlate_kernel, 1.0 / (groups * spectra), tile),
        in_specs=[pl.BlockSpec(memory_space=pltpu.VMEM)],
        out_specs=pl.BlockSpec(memory_space=pl.ANY),
        out_shape=jax.ShapeDtypeStruct((1, 2, total, total), jnp.float32),
        scratch_shapes=[
            pltpu.VMEM((2, total, total), jnp.float32),
            pltpu.SemaphoreType.DMA((blocks,)),
        ],
        compiler_params=pltpu.CompilerParams(vmem_limit_bytes=VMEM_BYTES),
        cost_estimate=pl.CostEstimate(
            flops=5 * total * total * groups * spectra,
            bytes_accessed=8 * total * total,
            transcendentals=0,
        ),
    )(signal)


def per_device(volts, taps):
    time_groups = lax.axis_size("tm")
    band_groups = lax.axis_size("band")
    taps_count, channels = taps.shape
    _, inputs, samples = volts.shape
    margin = (taps_count - 1) * channels
    history = shifted(volts[:, :, samples - margin :], "tm", 1)
    spectra = channelize(volts, history, taps, LANES)
    turned = lax.all_to_all(spectra, ("tm", "band"), split_axis=0, concat_axis=0, tiled=True)
    return correlate(turned.reshape(time_groups, band_groups, 2, inputs, samples // channels))


def solution(mesh):
    in_specs = (P(None, "band", "tm"), P())
    out_specs = P(("tm", "band"), None, None, None)
    return jax.shard_map(
        per_device, mesh=mesh, in_specs=in_specs, out_specs=out_specs, check_vma=False
    )
```

time: 226 us -> 149 us (0.66); the launches traced: 223 us -> 149 us
  blocking collectives: 160 us -> 116 us
  matrix products: 38.4 us -> 0 us
  Pallas kernels: 0 us -> 28.8 us
  local copies, waits for them, and re-layouts: 13.7 us -> 1.54 us
  other arithmetic: 8.91 us -> 0 us
    all_to_all x2 -> x1, blocking collectives: 160 us -> 116 us  [per_device(): lax.all_to_all(spectra, ('tm', 'band'), split_axis=0, concat_axis=0, tile...]
    dot_general x2 -> x0, matrix products: 38.4 us -> none  [the longest x1 27 us: per_device(): lax.dot_general(table, filtered, (((1, 2), (0, 3)), ((), ())), preferred_...]
    pallas_call x0 -> x2, Pallas kernels: none -> 28.8 us  [the longest x1 17.5 us: channelize(): pl.pallas_call(channelize_kernel, grid=(spectra // block,), in_specs=[pl....]
    convert_element_type x2 -> x0, local copies, waits for them, and re-layouts: 7.72 us -> none  [the longest x1 7.52 us: per_device(): frames.reshape(2, local_inputs, spec_local + taps_count - 1, channels)]
    convert_element_type x1 -> x0, other arithmetic: 6.06 us -> none  [per_device(): frames.reshape(2, local_inputs, spec_local + taps_count - 1, channels)]
    another operation x5 -> x0, other arithmetic: 2.58 us -> none
    reshape x1 -> x0, local copies, waits for them, and re-layouts: 2.37 us -> none  [per_device(): spectra.astype(jnp.bfloat16)]
  transfers between devices with their start and end apart: 1 -> 1, of which waited for: 0 -> 1; matrix products, arithmetic and copies ran while one was open for 2% -> 0% of each run, Pallas kernels for 0% -> 0%
where the time goes in v1:
time: 149 us
  blocking collectives  116 us (78%)
  Pallas kernels  28.8 us (19%)
  starting transfers between devices  1.73 us (1%)
  local copies, waits for them, and re-layouts  1.54 us (1%)
    all_to_all x1, blocking collectives, per_device(): lax.all_to_all(spectra, ('tm', 'band'), split_axis=0, concat_axis=0, tile...  116 us
    pallas_call x1, Pallas kernels, channelize(): pl.pallas_call(channelize_kernel, grid=(spectra // block,), in_specs=[pl....  17.5 us
    pallas_call x1, Pallas kernels, correlate(): pl.pallas_call(functools.partial(correlate_kernel, 1.0 / (groups * spectr...  11.3 us
  transfers between devices with their start and end apart: 1, of which 1 were waited for; matrix products, arithmetic and copies ran while one was open for 0% of the time, Pallas kernels for 0%

profile of v1, /device:TPU:6, one launch (start us, length us, event | category | flops | bytes accessed | tf_op | source)
XLA Modules:
  0.0 148.9 jit_solution(4853788412390974071)
XLA Ops:
  0.0 0.9 slice.3
  0.9 1.7 %collective-permute-start = (bf16[2,16,1792]{2,1,0:T(8,128)(2,1)S(1)}, bf16[2,16,1792]{2,1,0:T(8,128)(2,1)S(1)}, u32[]{:S(2)}, u32[]{:S(2)}) collective-permute-start(bf16[2,16,1792]{2,1,0:T(8,128)(2,1)S(1)} %slice.3), channel_id=1, source_target_pairs={{0,64},{64,128},{128,192},{1,65},{65,129},{129,193},{2,66},{66,130... | collective-permute-start | bytes 344072 | tf_op jit(solution)/shard_map/ppermute | solution.py:20
  2.6 0.9 collective-permute-done.history_ref
  3.6 0.0 copy-start
  3.6 0.6 copy-done
  4.2 17.5 %shard_map.37 = bf16[256,2,16,256]{3,2,1,0:T(8,128)(2,1)} custom-call(bf16[2,16,65536]{2,1,0:T(8,128)(2,1)} %volts_ref.1, bf16[2,16,1792]{2,1,0:T(8,128)(2,1)} %copy-done, f32[8,256]{1,0:T(8,128)} %taps_ref.1, bf16[512,512]{1,0:T(8,128)(2,1)} %constant.2.clone.table_ref), custom_call_target="tpu_custom_call" | custom-call | flops 2181038080 | bytes 16777216 | tf_op jit(solution)/shard_map/pallas_call | solution.py:89
  21.7 115.8 %all_to_all.5 = bf16[256,2,16,256]{3,2,1,0:T(8,128)(2,1)} all-to-all(bf16[256,2,16,256]{3,2,1,0:T(8,128)(2,1)} %shard_map.37), channel_id=1, replica_groups=mesh['tm'=4,'band'=64] {'tm','band'}, dimensions={0} | all-to-all | bytes 8388608 | tf_op jit(solution)/shard_map/all_to_all | solution.py:185
  137.5 11.3 %shard_map.38 = f32[1,2,1024,1024]{3,2,1,0:T(8,128)} custom-call(bf16[4,64,2,16,256]{4,3,2,1,0:T(8,128)(2,1)} %bitcast.1), custom_call_target="tpu_custom_call" | custom-call | flops 5368709120 | bytes 8388608 | tf_op jit(solution)/shard_map/pallas_call | solution.py:159
Async XLA Ops:
  0.9 2.7 %collective-permute-start = (bf16[2,16,1792]{2,1,0:T(8,128)(2,1)S(1)}, bf16[2,16,1792]{2,1,0:T(8,128)(2,1)S(1)}, u32[]{:S(2)}, u32[]{:S(2)}) collective-permute-start(bf16[2,16,1792]{2,1,0:T(8,128)(2,1)S(1)} %slice.3), channel_id=1, source_target_pairs={{0,64},{64,128},{128,192},{1,65},{65,129},{129,193},{2,66},{66,130... | collective-permute-start | bytes 344072 | tf_op jit(solution)/shard_map/ppermute | solution.py:20
  3.6 0.6 copy-start

commit v2 on v1

v2 whole, which is shorter than its diff:
```python
import functools
import math

import jax
import jax.numpy as jnp
import ml_dtypes
import numpy as np
from jax import lax
from jax.experimental import pallas as pl
from jax.experimental.pallas import tpu as pltpu
from jax.sharding import PartitionSpec as P

LANES = 128
SPARE = 8
VMEM_BYTES = 56 * 1024 * 1024


def dft_table(channels):
    index = np.arange(channels)
    theta = (index[:, None] * index[None, :] % channels) * (2.0 * math.pi / channels)
    factor = 1.0 / math.sqrt(channels)
    cosine = np.cos(theta) * factor
    sine = np.sin(theta) * factor
    real_row = np.stack([cosine, sine], axis=1)
    imag_row = np.stack([-sine, cosine], axis=1)
    table = np.stack([real_row, imag_row], axis=1)
    return table.reshape(2 * channels, 2 * channels).astype(np.float32).astype(ml_dtypes.bfloat16)


def filter_steps(volts, history, taps_ref, rows, pieces):
    taps_count, channels = taps_ref.shape
    inputs = volts.shape[1]
    block = volts.shape[2] // channels
    margin = taps_count - 1
    for part in range(2):
        for left in range(0, channels, LANES):
            weights = [taps_ref[j : j + 1, left : left + LANES] for j in range(taps_count)]

            def frame(index):
                if index < margin:
                    at = (index + 1) * channels + left
                    return history[part, :, at : at + LANES].astype(jnp.float32)
                at = (index - margin) * channels + left
                return volts[part, :, at : at + LANES].astype(jnp.float32)

            window = [frame(index) for index in range(margin)]
            for t in range(block):
                window.append(frame(t + margin))
                terms = [weights[j] * window[j] for j in range(taps_count)]
                while len(terms) > 1:
                    terms = [terms[n] + terms[n + 1] for n in range(0, len(terms), 2)]
                rows[(part * channels + left) // LANES, pl.ds(t, inputs, stride=block + SPARE), :] = terms[0]
                window = window[1:]
                if (t + 1) % (block // pieces) == 0:
                    yield


def dft_steps(table_ref, rows, turned, inputs, together):
    bins = table_ref.shape[0]
    block = LANES
    pitch = rows.shape[1] // inputs
    for step in range(inputs // together):
        signal = jnp.concatenate(
            [
                jnp.concatenate([rows[n, i * pitch : i * pitch + block, :].astype(jnp.bfloat16) for n in range(rows.shape[0])], axis=1)
                for i in range(step * together, (step + 1) * together)
            ],
            axis=0,
        )
        found = lax.dot_general(
            table_ref[...], signal, (((1,), (1,)), ((), ())), preferred_element_type=jnp.float32
        )
        for n in range(together):
            turned[pl.ds(step * together + n, bins, stride=inputs + SPARE), :] = found[:, n * block : (n + 1) * block]
        yield


def filter_kernel(volts_ref, history_ref, taps_ref, out_ref, rows):
    for _ in filter_steps(volts_ref, history_ref, taps_ref, rows, 1):
        pass
    inputs = volts_ref.shape[1]
    for i in range(inputs):
        first = i * (LANES + SPARE)
        out_ref[:, i * LANES : (i + 1) * LANES] = rows[:, first : first + LANES].astype(jnp.bfloat16)


def without_spare(turned, inputs):
    block = turned.shape[1]
    return turned[...].reshape(-1, inputs + SPARE, block)[:, :inputs].astype(jnp.bfloat16)


def channelize_kernel(
    filtered_ref, volts_ref, history_ref, taps_ref, table_ref, out_ref, rows, turned, late, early, sems
):
    inputs = volts_ref.shape[1]
    block = LANES
    steps = filter_steps(volts_ref, history_ref, taps_ref, rows, 2)
    for _ in dft_steps(table_ref, filtered_ref, turned, inputs, 2):
        next(steps)
    late[...] = without_spare(turned, inputs).reshape(late.shape)
    sent = [pltpu.make_async_copy(late, out_ref.at[:, :, :, pl.ds(block, block)], sems.at[0])]
    sent[0].start()
    for _ in dft_steps(table_ref, rows, turned, inputs, 2):
        pass
    early[...] = without_spare(turned, inputs).reshape(early.shape)
    sent.append(pltpu.make_async_copy(early, out_ref.at[:, :, :, pl.ds(0, block)], sems.at[1]))
    sent[1].start()
    for copy in sent:
        copy.wait()


def channelize(volts, history, taps):
    taps_count, channels = taps.shape
    _, inputs, samples = volts.shape
    spectra = samples // channels
    block = LANES
    reach = taps_count * channels
    halves = pl.BlockSpec((2, inputs, block * channels), lambda n: (0, 0, 1))
    tiles = 2 * channels // LANES
    rows = (tiles, inputs * block, LANES)
    spaced = (tiles, inputs * (block + SPARE), LANES)
    params = pltpu.CompilerParams(vmem_limit_bytes=VMEM_BYTES)
    filtered = pl.pallas_call(
        filter_kernel,
        grid=(1,),
        in_specs=[
            halves,
            pl.BlockSpec((2, inputs, reach), lambda n: (0, 0, block // taps_count - 1)),
            pl.BlockSpec(taps.shape, lambda n: (0, 0)),
        ],
        out_specs=pl.BlockSpec(rows, lambda n: (0, 0, 0)),
        out_shape=jax.ShapeDtypeStruct(rows, jnp.bfloat16),
        scratch_shapes=[pltpu.VMEM(spaced, jnp.float32)],
        compiler_params=params,
        cost_estimate=pl.CostEstimate(
            flops=4 * taps_count * block * inputs * channels,
            bytes_accessed=8 * block * inputs * channels,
            transcendentals=0,
        ),
    )(volts, volts, taps)
    return pl.pallas_call(
        channelize_kernel,
        grid=(1,),
        in_specs=[
            pl.BlockSpec(rows, lambda n: (0, 0, 0)),
            pl.BlockSpec((2, inputs, block * channels), lambda n: (0, 0, 0)),
            pl.BlockSpec(history.shape, lambda n: (0, 0, 0)),
            pl.BlockSpec(taps.shape, lambda n: (0, 0)),
            pl.BlockSpec((2 * channels, 2 * channels), lambda n: (0, 0)),
        ],
        out_specs=pl.BlockSpec(memory_space=pl.ANY),
        out_shape=jax.ShapeDtypeStruct((channels, 2, inputs, spectra), jnp.bfloat16),
        scratch_shapes=[
            pltpu.VMEM(spaced, jnp.float32),
            pltpu.VMEM((2 * channels * (inputs + SPARE), block), jnp.float32),
            pltpu.VMEM((channels, 2, inputs, block), jnp.bfloat16),
            pltpu.VMEM((channels, 2, inputs, block), jnp.bfloat16),
            pltpu.SemaphoreType.DMA((2,)),
        ],
        compiler_params=params,
        cost_estimate=pl.CostEstimate(
            flops=8 * spectra * inputs * channels * channels,
            bytes_accessed=12 * spectra * inputs * channels,
            transcendentals=0,
        ),
    )(filtered, volts, history, taps, jnp.asarray(dft_table(channels)))


def correlate_kernel(scale, tile, signal_ref, out_ref, here, plain, crossed, store, in_sems, out_sems):
    groups, bands, _, inputs, times = signal_ref.shape
    total = bands * inputs
    half_depth = groups * times
    arriving = [pltpu.make_async_copy(signal_ref.at[g], here.at[g], in_sems.at[g]) for g in range(groups)]
    for copy in arriving:
        copy.start()
    for g in range(groups):
        arriving[g].wait()
        real = here[g, :, 0].reshape(total, times)
        imag = here[g, :, 1].reshape(total, times)
        low, high = g * times, half_depth + g * times
        plain[:, low : low + times] = real
        plain[:, high : high + times] = imag
        crossed[:, low : low + times] = imag
        crossed[:, high : high + times] = -real

    contract = (((1,), (1,)), ((), ()))
    copies = []

    def send(p, rows, q, columns):
        where = (slice(None), pl.ds(p, rows), pl.ds(q, columns))
        copy = pltpu.make_async_copy(store.at[where], out_ref.at[(0, *where)], out_sems.at[len(copies)])
        copy.start()
        copies.append(copy)

    for q in range(0, total, tile):
        right = plain[q : q + tile, :]
        real = lax.dot_general(plain[q:, :], right, contract, preferred_element_type=jnp.float32) * scale
        imag = lax.dot_general(crossed[q:, :], right, contract, preferred_element_type=jnp.float32) * scale
        store[0, q:, q : q + tile] = real
        store[1, q:, q : q + tile] = imag
        send(q, total - q, q, tile)
        if q + tile < total:
            store[0, q : q + tile, q + tile :] = real[tile:].T
            store[1, q : q + tile, q + tile :] = -(imag[tile:].T)
            send(q, tile, q + tile, total - q - tile)
    for copy in copies:
        copy.wait()


def correlate(signal):
    groups, bands, _, inputs, times = signal.shape
    total = bands * inputs
    spectra = groups * times
    tile = 256
    return pl.pallas_call(
        functools.partial(correlate_kernel, 1.0 / spectra, tile),
        in_specs=[pl.BlockSpec(memory_space=pl.ANY)],
        out_specs=pl.BlockSpec(memory_space=pl.ANY),
        out_shape=jax.ShapeDtypeStruct((1, 2, total, total), jnp.float32),
        scratch_shapes=[
            pltpu.VMEM(signal.shape, jnp.bfloat16),
            pltpu.VMEM((total, 2 * spectra), jnp.bfloat16),
            pltpu.VMEM((total, 2 * spectra), jnp.bfloat16),
            pltpu.VMEM((2, total, total), jnp.float32),
            pltpu.SemaphoreType.DMA((groups,)),
            pltpu.SemaphoreType.DMA((2 * (total // tile) - 1,)),
        ],
        compiler_params=pltpu.CompilerParams(vmem_limit_bytes=VMEM_BYTES),
        cost_estimate=pl.CostEstimate(
            flops=5 * total * total * spectra, bytes_accessed=12 * total * total, transcendentals=0
        ),
    )(signal)


def per_device(volts, taps):
    time_groups = lax.axis_size("tm")
    band_groups = lax.axis_size("band")
    taps_count, channels = taps.shape
    _, inputs, samples = volts.shape
    reach = taps_count * channels
    history = lax.ppermute(volts[:, :, samples - reach :], "tm", [(i, i + 1) for i in range(time_groups - 1)])
    spectra = channelize(volts, history, taps)
    turned = lax.all_to_all(spectra, ("tm", "band"), split_axis=0, concat_axis=0, tiled=True)
    return correlate(turned.reshape(time_groups, band_groups, 2, inputs, samples // channels))


def solution(mesh):
    in_specs = (P(None, "band", "tm"), P())
    out_specs = P(("tm", "band"), None, None, None)
    return jax.shard_map(
        per_device, mesh=mesh, in_specs=in_specs, out_specs=out_specs, check_vma=False
    )
```

time: 149 us -> 141 us (0.946)
  Pallas kernels: 28.8 us -> 23.6 us
  blocking collectives: 116 us -> 114 us
    pallas_call x2 -> x3, Pallas kernels: 28.8 us -> 23.6 us  [the longest x1 9.42 us: correlate(): pl.pallas_call(functools.partial(correlate_kernel, 1.0 / spectra, tile),...]
    all_to_all x1, blocking collectives: 116 us -> 114 us  [per_device(): lax.all_to_all(spectra, ('tm', 'band'), split_axis=0, concat_axis=0, tile...]
  transfers between devices with their start and end apart: 1 -> 1, of which waited for: 1 -> 0; matrix products, arithmetic and copies ran while one was open for 0% -> 0% of each run, Pallas kernels for 0% -> 4%
where the time goes in v2:
time: 141 us
  blocking collectives  114 us (81%)
  Pallas kernels  23.6 us (17%)
  starting transfers between devices  1.75 us (1%)
  local copies, waits for them, and re-layouts  1.57 us (1%)
    all_to_all x1, blocking collectives, per_device(): lax.all_to_all(spectra, ('tm', 'band'), split_axis=0, concat_axis=0, tile...  114 us
    pallas_call x1, Pallas kernels, correlate(): pl.pallas_call(functools.partial(correlate_kernel, 1.0 / spectra, tile),...  9.42 us
    pallas_call x1, Pallas kernels, channelize(): pl.pallas_call(channelize_kernel, grid=(1,), in_specs=[pl.BlockSpec(rows,...  8.82 us
    pallas_call x1, Pallas kernels, channelize(): pl.pallas_call(filter_kernel, grid=(1,), in_specs=[halves, pl.BlockSpec((...  5.38 us
  transfers between devices with their start and end apart: 1, of which 0 were waited for; matrix products, arithmetic and copies ran while one was open for 0% of the time, Pallas kernels for 4%

profile of v2, /device:TPU:6, one launch (start us, length us, event | category | flops | bytes accessed | tf_op | source)
XLA Modules:
  0.0 140.9 jit_solution(15054247562218315194)
XLA Ops:
  0.0 0.9 slice.3
  0.9 1.7 %collective-permute-start = (bf16[2,16,2048]{2,1,0:T(8,128)(2,1)S(1)}, bf16[2,16,2048]{2,1,0:T(8,128)(2,1)S(1)}, u32[]{:S(2)}, u32[]{:S(2)}) collective-permute-start(bf16[2,16,2048]{2,1,0:T(8,128)(2,1)S(1)} %slice.3), channel_id=1, source_target_pairs={{0,64},{64,128},{128,192},{1,65},{65,129},{129,193},{2,66},{66,130... | collective-permute-start | bytes 393224 | tf_op jit(solution)/shard_map/ppermute | solution.py:241
  2.7 5.4 %shard_map.37.filtered_ref = bf16[4,2048,128]{2,1,0:T(8,128)(2,1)} custom-call(bf16[2,16,65536]{2,1,0:T(8,128)(2,1)} %volts_ref.3, bf16[2,16,65536]{2,1,0:T(8,128)(2,1)} %volts_ref.3, f32[8,256]{1,0:T(8,128)} %taps_ref.3), custom_call_target="tpu_custom_call" | custom-call | flops 16777216 | bytes 4194304 | tf_op jit(solution)/shard_map/pallas_call | solution.py:123
  8.1 0.0 collective-permute-done.history_ref
  8.1 0.0 copy-start
  8.1 0.7 copy-done
  8.7 8.8 %shard_map.38 = bf16[256,2,16,256]{3,2,1,0:T(8,128)(2,1)} custom-call(bf16[4,2048,128]{2,1,0:T(8,128)(2,1)} %shard_map.37.filtered_ref, bf16[2,16,65536]{2,1,0:T(8,128)(2,1)} %volts_ref.3, bf16[2,16,2048]{2,1,0:T(8,128)(2,1)} %copy-done, f32[8,256]{1,0:T(8,128)} %taps_ref.3, bf16[512,512]{1,0:T(8,128)(2,1)} %constant.2.clone.table_ref), custom_call_target="tpu_custom_call" | custom-call | flops 2147483648 | bytes 12582912 | tf_op jit(solution)/shard_map/pallas_call | solution.py:141
  17.6 113.8 %all_to_all.5 = bf16[256,2,16,256]{3,2,1,0:T(8,128)(2,1)} all-to-all(bf16[256,2,16,256]{3,2,1,0:T(8,128)(2,1)} %shard_map.38), channel_id=1, replica_groups=mesh['tm'=4,'band'=64] {'tm','band'}, dimensions={0} | all-to-all | bytes 8388608 | tf_op jit(solution)/shard_map/all_to_all | solution.py:243
  131.3 9.4 %shard_map.39 = f32[1,2,1024,1024]{3,2,1,0:T(8,128)} custom-call(bf16[4,64,2,16,256]{4,3,2,1,0:T(8,128)(2,1)} %bitcast.1), custom_call_target="tpu_custom_call" | custom-call | flops 5368709120 | bytes 12582912 | tf_op jit(solution)/shard_map/pallas_call | solution.py:215
Async XLA Ops:
  0.9 7.1 %collective-permute-start = (bf16[2,16,2048]{2,1,0:T(8,128)(2,1)S(1)}, bf16[2,16,2048]{2,1,0:T(8,128)(2,1)S(1)}, u32[]{:S(2)}, u32[]{:S(2)}) collective-permute-start(bf16[2,16,2048]{2,1,0:T(8,128)(2,1)S(1)} %slice.3), channel_id=1, source_target_pairs={{0,64},{64,128},{128,192},{1,65},{65,129},{129,193},{2,66},{66,130... | collective-permute-start | bytes 393224 | tf_op jit(solution)/shard_map/ppermute | solution.py:241
  8.1 0.7 copy-start

commit v3 on v2

v3 whole, which is shorter than its diff:
```python
import functools
import math

import jax
import jax.numpy as jnp
import ml_dtypes
import numpy as np
from jax import lax
from jax.experimental import pallas as pl
from jax.experimental.pallas import tpu as pltpu
from jax.sharding import PartitionSpec as P

LANES = 128
SPARE = 8
VMEM_BYTES = 56 * 1024 * 1024


def dft_table(channels):
    index = np.arange(channels)
    theta = (index[:, None] * index[None, :] % channels) * (2.0 * math.pi / channels)
    factor = 1.0 / math.sqrt(channels)
    cosine = np.cos(theta) * factor
    sine = np.sin(theta) * factor
    real_row = np.stack([cosine, sine], axis=1)
    imag_row = np.stack([-sine, cosine], axis=1)
    table = np.stack([real_row, imag_row], axis=1)
    return table.reshape(2 * channels, 2 * channels).astype(np.float32).astype(ml_dtypes.bfloat16)


def filter_steps(volts, history, taps_ref, rows, pieces):
    taps_count, channels = taps_ref.shape
    inputs = volts.shape[1]
    block = volts.shape[2] // channels
    margin = taps_count - 1
    for part in range(2):
        for left in range(0, channels, LANES):
            weights = [taps_ref[j : j + 1, left : left + LANES] for j in range(taps_count)]

            def frame(index):
                if index < margin:
                    at = (index + 1) * channels + left
                    return history[part, :, at : at + LANES].astype(jnp.float32)
                at = (index - margin) * channels + left
                return volts[part, :, at : at + LANES].astype(jnp.float32)

            window = [frame(index) for index in range(margin)]
            for t in range(block):
                window.append(frame(t + margin))
                terms = [weights[j] * window[j] for j in range(taps_count)]
                while len(terms) > 1:
                    terms = [terms[n] + terms[n + 1] for n in range(0, len(terms), 2)]
                rows[(part * channels + left) // LANES, pl.ds(t, inputs, stride=block + SPARE), :] = terms[0]
                window = window[1:]
                if (t + 1) % (block // pieces) == 0:
                    yield


def dft_steps(table_ref, rows, turned, inputs, together):
    bins = table_ref.shape[0]
    block = LANES
    pitch = rows.shape[1] // inputs
    for step in range(inputs // together):
        signal = jnp.concatenate(
            [
                jnp.concatenate([rows[n, i * pitch : i * pitch + block, :].astype(jnp.bfloat16) for n in range(rows.shape[0])], axis=1)
                for i in range(step * together, (step + 1) * together)
            ],
            axis=0,
        )
        found = lax.dot_general(
            table_ref[...], signal, (((1,), (1,)), ((), ())), preferred_element_type=jnp.float32
        )
        for n in range(together):
            turned[pl.ds(step * together + n, bins, stride=inputs + SPARE), :] = found[:, n * block : (n + 1) * block]
        yield


def rounding_steps(turned, out, inputs, pieces):
    channels, _, _, block = out.shape
    part = channels // pieces
    pitch = inputs + SPARE
    for n in range(pieces):
        found = turned[2 * n * part * pitch : 2 * (n + 1) * part * pitch, :].reshape(2 * part, pitch, block)
        out[n * part : (n + 1) * part] = found[:, :inputs].astype(jnp.bfloat16).reshape(part, 2, inputs, block)
        yield pl.ds(n * part, part)


def channelize_kernel(
    volts_ref, history_ref, taps_ref, table_ref, out_ref, volts, before, rows, turned, rounded, in_sems, out_sems
):
    inputs = volts_ref.shape[1]
    taps_count, channels = taps_ref.shape
    block = LANES
    width = block * channels
    reach = taps_count * channels
    ahead = pltpu.make_async_copy(volts_ref.at[:, :, pl.ds(width - reach, reach)], before, in_sems.at[2, 0])
    ahead.start()
    arriving = {}
    for half in (1, 0):
        for part in range(2):
            copy = pltpu.make_async_copy(
                volts_ref.at[part, :, pl.ds(half * width, width)], volts.at[half, part], in_sems.at[half, part]
            )
            copy.start()
            arriving[half, part] = copy

    pieces = 4
    ahead.wait()
    arriving[1, 0].wait()
    late = filter_steps(volts.at[1], before, taps_ref, rows.at[1], pieces)
    for n in range(2 * channels // LANES * pieces):
        if n == channels // LANES * pieces:
            arriving[1, 1].wait()
        next(late)
    arriving[0, 0].wait()
    arriving[0, 1].wait()
    early = filter_steps(volts.at[0], history_ref, taps_ref, rows.at[0], pieces)
    for _ in dft_steps(table_ref, rows.at[1], turned.at[1], inputs, 2):
        next(early)
        next(early)
    sent = []

    def send(half, where):
        copy = pltpu.make_async_copy(
            rounded.at[half, where], out_ref.at[where, :, :, pl.ds(half * block, block)], out_sems.at[len(sent)]
        )
        copy.start()
        sent.append(copy)

    steps = dft_steps(table_ref, rows.at[0], turned.at[0], inputs, 2)
    for where in rounding_steps(turned.at[1], rounded.at[1], inputs, inputs // 2):
        send(1, where)
        next(steps)
    for where in rounding_steps(turned.at[0], rounded.at[0], inputs, 4):
        send(0, where)
    for copy in sent:
        copy.wait()


def channelize(volts, history, taps):
    taps_count, channels = taps.shape
    _, inputs, samples = volts.shape
    spectra = samples // channels
    block = LANES
    resident = pl.BlockSpec(memory_space=pltpu.VMEM)
    return pl.pallas_call(
        channelize_kernel,
        in_specs=[pl.BlockSpec(memory_space=pl.ANY), resident, resident, resident],
        out_specs=pl.BlockSpec(memory_space=pl.ANY),
        out_shape=jax.ShapeDtypeStruct((channels, 2, inputs, spectra), jnp.bfloat16),
        scratch_shapes=[
            pltpu.VMEM((2, 2, inputs, block * channels), jnp.bfloat16),
            pltpu.VMEM((2, inputs, taps_count * channels), jnp.bfloat16),
            pltpu.VMEM((2, 2 * channels // LANES, inputs * (block + SPARE), LANES), jnp.float32),
            pltpu.VMEM((2, 2 * channels * (inputs + SPARE), block), jnp.float32),
            pltpu.VMEM((2, channels, 2, inputs, block), jnp.bfloat16),
            pltpu.SemaphoreType.DMA((3, 2)),
            pltpu.SemaphoreType.DMA((inputs // 2 + 4,)),
        ],
        compiler_params=pltpu.CompilerParams(vmem_limit_bytes=VMEM_BYTES),
        cost_estimate=pl.CostEstimate(
            flops=8 * spectra * inputs * channels * channels,
            bytes_accessed=8 * spectra * inputs * channels,
            transcendentals=0,
        ),
    )(volts, history, taps, jnp.asarray(dft_table(channels)))


def correlate_kernel(scale, tile, signal_ref, out_ref, here, plain, crossed, store, in_sems, out_sems):
    groups, bands, _, inputs, times = signal_ref.shape
    total = bands * inputs
    half_depth = groups * times
    width = tile // inputs
    arriving = []
    for n in range(total // tile):
        where = (slice(None), pl.ds(n * width, width))
        arriving.append(pltpu.make_async_copy(signal_ref.at[where], here.at[where], in_sems.at[n]))
        arriving[n].start()

    contract = (((1,), (1,)), ((), ()))
    copies = []

    def put(p, q, real, imag):
        where = (slice(None), pl.ds(p, tile), pl.ds(q, tile))
        store[0, p : p + tile, q : q + tile] = real
        store[1, p : p + tile, q : q + tile] = imag
        copy = pltpu.make_async_copy(store.at[where], out_ref.at[(0, *where)], out_sems.at[len(copies)])
        copy.start()
        copies.append(copy)

    for n in range(total // tile):
        arriving[n].wait()
        p = n * tile
        for g in range(groups):
            real = here[g, n * width : (n + 1) * width, 0].reshape(tile, times)
            imag = here[g, n * width : (n + 1) * width, 1].reshape(tile, times)
            low, high = g * times, half_depth + g * times
            plain[p : p + tile, low : low + times] = real
            plain[p : p + tile, high : high + times] = imag
            crossed[p : p + tile, low : low + times] = imag
            crossed[p : p + tile, high : high + times] = -real
        for q in range(0, p + tile, tile):
            right = plain[q : q + tile, :]
            real = lax.dot_general(plain[p : p + tile, :], right, contract, preferred_element_type=jnp.float32) * scale
            imag = lax.dot_general(crossed[p : p + tile, :], right, contract, preferred_element_type=jnp.float32) * scale
            put(p, q, real, imag)
            if p != q:
                put(q, p, real.T, -imag.T)
    for copy in copies:
        copy.wait()


def correlate(signal):
    groups, bands, _, inputs, times = signal.shape
    total = bands * inputs
    spectra = groups * times
    tile = 256
    return pl.pallas_call(
        functools.partial(correlate_kernel, 1.0 / spectra, tile),
        in_specs=[pl.BlockSpec(memory_space=pl.ANY)],
        out_specs=pl.BlockSpec(memory_space=pl.ANY),
        out_shape=jax.ShapeDtypeStruct((1, 2, total, total), jnp.float32),
        scratch_shapes=[
            pltpu.VMEM(signal.shape, jnp.bfloat16),
            pltpu.VMEM((total, 2 * spectra), jnp.bfloat16),
            pltpu.VMEM((total, 2 * spectra), jnp.bfloat16),
            pltpu.VMEM((2, total, total), jnp.float32),
            pltpu.SemaphoreType.DMA((total // tile,)),
            pltpu.SemaphoreType.DMA(((total // tile) ** 2,)),
        ],
        compiler_params=pltpu.CompilerParams(vmem_limit_bytes=VMEM_BYTES),
        cost_estimate=pl.CostEstimate(
            flops=5 * total * total * spectra, bytes_accessed=12 * total * total, transcendentals=0
        ),
    )(signal)


def per_device(volts, taps):
    time_groups = lax.axis_size("tm")
    band_groups = lax.axis_size("band")
    taps_count, channels = taps.shape
    _, inputs, samples = volts.shape
    reach = taps_count * channels
    history = lax.ppermute(volts[:, :, samples - reach :], "tm", [(i, i + 1) for i in range(time_groups - 1)])
    spectra = channelize(volts, history, taps)
    turned = lax.all_to_all(spectra, ("tm", "band"), split_axis=0, concat_axis=0, tiled=True)
    return correlate(turned.reshape(time_groups, band_groups, 2, inputs, samples // channels))


def solution(mesh):
    in_specs = (P(None, "band", "tm"), P())
    out_specs = P(("tm", "band"), None, None, None)
    return jax.shard_map(
        per_device, mesh=mesh, in_specs=in_specs, out_specs=out_specs, check_vma=False
    )
```

time: 141 us -> 140 us (level)
  Pallas kernels: 23.6 us -> 19.6 us
  blocking collectives: 114 us -> 116 us
    pallas_call x2 -> x1, Pallas kernels: 14.2 us -> 10.9 us  [channelize(): pl.pallas_call(channelize_kernel, in_specs=[pl.BlockSpec(memory_space=pl....]
    all_to_all x1, blocking collectives: 114 us -> 116 us  [per_device(): lax.all_to_all(spectra, ('tm', 'band'), split_axis=0, concat_axis=0, tile...]
  transfers between devices with their start and end apart: 1 -> 1, of which waited for: 0 -> 1; matrix products, arithmetic and copies ran while one was open for 0% -> 0% of each run, Pallas kernels for 4% -> 0%
where the time goes in v3:
time: 140 us
  blocking collectives  116 us (83%)
  Pallas kernels  19.6 us (14%)
  starting transfers between devices  1.75 us (1%)
  local copies, waits for them, and re-layouts  1.55 us (1%)
    all_to_all x1, blocking collectives, per_device(): lax.all_to_all(spectra, ('tm', 'band'), split_axis=0, concat_axis=0, tile...  116 us
    pallas_call x1, Pallas kernels, channelize(): pl.pallas_call(channelize_kernel, in_specs=[pl.BlockSpec(memory_space=pl....  10.9 us
    pallas_call x1, Pallas kernels, correlate(): pl.pallas_call(functools.partial(correlate_kernel, 1.0 / spectra, tile),...  8.74 us
  transfers between devices with their start and end apart: 1, of which 1 were waited for; matrix products, arithmetic and copies ran while one was open for 0% of the time, Pallas kernels for 0%

profile of v3, /device:TPU:6, one launch (start us, length us, event | category | flops | bytes accessed | tf_op | source)
XLA Modules:
  0.0 140.0 jit_solution(10848110374938175845)
XLA Ops:
  0.0 0.9 slice.3
  0.9 1.7 %collective-permute-start = (bf16[2,16,2048]{2,1,0:T(8,128)(2,1)S(1)}, bf16[2,16,2048]{2,1,0:T(8,128)(2,1)S(1)}, u32[]{:S(2)}, u32[]{:S(2)}) collective-permute-start(bf16[2,16,2048]{2,1,0:T(8,128)(2,1)S(1)} %slice.3), channel_id=1, source_target_pairs={{0,64},{64,128},{128,192},{1,65},{65,129},{129,193},{2,66},{66,130... | collective-permute-start | bytes 393224 | tf_op jit(solution)/shard_map/ppermute | solution.py:244
  2.7 1.0 collective-permute-done.history_ref
  3.6 0.0 copy-start
  3.6 0.6 copy-done
  4.3 10.9 %shard_map.37 = bf16[256,2,16,256]{3,2,1,0:T(8,128)(2,1)} custom-call(bf16[2,16,65536]{2,1,0:T(8,128)(2,1)} %volts_ref.1, bf16[2,16,2048]{2,1,0:T(8,128)(2,1)} %copy-done, f32[8,256]{1,0:T(8,128)} %taps_ref.1, bf16[512,512]{1,0:T(8,128)(2,1)} %constant.2.clone.table_ref), custom_call_target="tpu_custom_call" | custom-call | flops 2147483648 | bytes 8388608 | tf_op jit(solution)/shard_map/pallas_call | solution.py:146
  15.2 116.0 %all_to_all.5 = bf16[256,2,16,256]{3,2,1,0:T(8,128)(2,1)} all-to-all(bf16[256,2,16,256]{3,2,1,0:T(8,128)(2,1)} %shard_map.37), channel_id=1, replica_groups=mesh['tm'=4,'band'=64] {'tm','band'}, dimensions={0} | all-to-all | bytes 8388608 | tf_op jit(solution)/shard_map/all_to_all | solution.py:246
  131.2 8.7 %shard_map.38 = f32[1,2,1024,1024]{3,2,1,0:T(8,128)} custom-call(bf16[4,64,2,16,256]{4,3,2,1,0:T(8,128)(2,1)} %bitcast.1), custom_call_target="tpu_custom_call" | custom-call | flops 5368709120 | bytes 12582912 | tf_op jit(solution)/shard_map/pallas_call | solution.py:218
Async XLA Ops:
  0.9 2.7 %collective-permute-start = (bf16[2,16,2048]{2,1,0:T(8,128)(2,1)S(1)}, bf16[2,16,2048]{2,1,0:T(8,128)(2,1)S(1)}, u32[]{:S(2)}, u32[]{:S(2)}) collective-permute-start(bf16[2,16,2048]{2,1,0:T(8,128)(2,1)S(1)} %slice.3), channel_id=1, source_target_pairs={{0,64},{64,128},{128,192},{1,65},{65,129},{129,193},{2,66},{66,130... | collective-permute-start | bytes 393224 | tf_op jit(solution)/shard_map/ppermute | solution.py:244
  3.6 0.6 copy-start

commit v4 on v3

--- a/solution.py
+++ b/solution.py
@@ -13,6 +13,7 @@
 LANES = 128
 SPARE = 8
 VMEM_BYTES = 56 * 1024 * 1024
+LATE_VMEM_BYTES = 24 * 1024 * 1024
 
 
 def dft_table(channels):
@@ -166,17 +167,11 @@
     )(volts, history, taps, jnp.asarray(dft_table(channels)))
 
 
-def correlate_kernel(scale, tile, signal_ref, out_ref, here, plain, crossed, store, in_sems, out_sems):
-    groups, bands, _, inputs, times = signal_ref.shape
+def correlate_kernel(scale, tile, here, out_ref, plain, crossed, store, out_sems):
+    groups, bands, _, inputs, times = here.shape
     total = bands * inputs
     half_depth = groups * times
     width = tile // inputs
-    arriving = []
-    for n in range(total // tile):
-        where = (slice(None), pl.ds(n * width, width))
-        arriving.append(pltpu.make_async_copy(signal_ref.at[where], here.at[where], in_sems.at[n]))
-        arriving[n].start()
-
     contract = (((1,), (1,)), ((), ()))
     copies = []
 
@@ -189,7 +184,6 @@
         copies.append(copy)
 
     for n in range(total // tile):
-        arriving[n].wait()
         p = n * tile
         for g in range(groups):
             real = here[g, n * width : (n + 1) * width, 0].reshape(tile, times)
@@ -217,18 +211,16 @@
     tile = 256
     return pl.pallas_call(
         functools.partial(correlate_kernel, 1.0 / spectra, tile),
-        in_specs=[pl.BlockSpec(memory_space=pl.ANY)],
+        in_specs=[pl.BlockSpec(memory_space=pltpu.VMEM)],
         out_specs=pl.BlockSpec(memory_space=pl.ANY),
         out_shape=jax.ShapeDtypeStruct((1, 2, total, total), jnp.float32),
         scratch_shapes=[
-            pltpu.VMEM(signal.shape, jnp.bfloat16),
             pltpu.VMEM((total, 2 * spectra), jnp.bfloat16),
             pltpu.VMEM((total, 2 * spectra), jnp.bfloat16),
             pltpu.VMEM((2, total, total), jnp.float32),
-            pltpu.SemaphoreType.DMA((total // tile,)),
             pltpu.SemaphoreType.DMA(((total // tile) ** 2,)),
         ],
-        compiler_params=pltpu.CompilerParams(vmem_limit_bytes=VMEM_BYTES),
+        compiler_params=pltpu.CompilerParams(vmem_limit_bytes=LATE_VMEM_BYTES),
         cost_estimate=pl.CostEstimate(
             flops=5 * total * total * spectra, bytes_accessed=12 * total * total, transcendentals=0
         ),

time: 140 us -> 139 us (level)
  Pallas kernels: 19.6 us -> 18.2 us
    pallas_call x1, Pallas kernels: 8.74 us -> 7.27 us  [correlate(): pl.pallas_call(functools.partial(correlate_kernel, 1.0 / spectra, tile),...]
where the time goes in v4:
time: 139 us; the launch traced here: 138 us
  blocking collectives  116 us (83%)
  Pallas kernels  18.2 us (13%)
  starting transfers between devices  1.75 us (1%)
  local copies, waits for them, and re-layouts  1.55 us (1%)
    all_to_all x1, blocking collectives, per_device(): lax.all_to_all(spectra, ('tm', 'band'), split_axis=0, concat_axis=0, tile...  116 us
    pallas_call x1, Pallas kernels, channelize(): pl.pallas_call(channelize_kernel, in_specs=[pl.BlockSpec(memory_space=pl....  10.9 us
    pallas_call x1, Pallas kernels, correlate(): pl.pallas_call(functools.partial(correlate_kernel, 1.0 / spectra, tile),...  7.27 us
  transfers between devices with their start and end apart: 1, of which 1 were waited for; matrix products, arithmetic and copies ran while one was open for 0% of the time, Pallas kernels for 0%

profile of v4, /device:TPU:6, one launch (start us, length us, event | category | flops | bytes accessed | tf_op | source)
XLA Modules:
  0.0 138.5 jit_solution(4625376436089768675)
XLA Ops:
  0.0 0.9 slice.3
  0.9 1.7 %collective-permute-start = (bf16[2,16,2048]{2,1,0:T(8,128)(2,1)S(1)}, bf16[2,16,2048]{2,1,0:T(8,128)(2,1)S(1)}, u32[]{:S(2)}, u32[]{:S(2)}) collective-permute-start(bf16[2,16,2048]{2,1,0:T(8,128)(2,1)S(1)} %slice.3), channel_id=1, source_target_pairs={{0,64},{64,128},{128,192},{1,65},{65,129},{129,193},{2,66},{66,130... | collective-permute-start | bytes 393224 | tf_op jit(solution)/shard_map/ppermute | solution.py:236
  2.7 1.0 collective-permute-done.history_ref
  3.6 0.0 copy-start
  3.6 0.6 copy-done
  4.3 10.9 %shard_map.37 = bf16[256,2,16,256]{3,2,1,0:T(8,128)(2,1)} custom-call(bf16[2,16,65536]{2,1,0:T(8,128)(2,1)} %volts_ref.1, bf16[2,16,2048]{2,1,0:T(8,128)(2,1)} %copy-done, f32[8,256]{1,0:T(8,128)} %taps_ref.1, bf16[512,512]{1,0:T(8,128)(2,1)} %constant.2.clone.table_ref), custom_call_target="tpu_custom_call" | custom-call | flops 2147483648 | bytes 8388608 | tf_op jit(solution)/shard_map/pallas_call | solution.py:147
  15.2 115.9 %all_to_all.5 = bf16[256,2,16,256]{3,2,1,0:T(8,128)(2,1)S(1)} all-to-all(bf16[256,2,16,256]{3,2,1,0:T(8,128)(2,1)} %shard_map.37), channel_id=1, replica_groups=mesh['tm'=4,'band'=64] {'tm','band'}, dimensions={0} | all-to-all | bytes 8388608 | tf_op jit(solution)/shard_map/all_to_all | solution.py:238
  131.0 7.3 %shard_map.38 = f32[1,2,1024,1024]{3,2,1,0:T(8,128)} custom-call(bf16[4,64,2,16,256]{4,3,2,1,0:T(8,128)(2,1)S(1)} %bitcast.1), custom_call_target="tpu_custom_call" | custom-call | flops 5368709120 | bytes 12582912 | tf_op jit(solution)/shard_map/pallas_call | solution.py:212
Async XLA Ops:
  0.9 2.7 %collective-permute-start = (bf16[2,16,2048]{2,1,0:T(8,128)(2,1)S(1)}, bf16[2,16,2048]{2,1,0:T(8,128)(2,1)S(1)}, u32[]{:S(2)}, u32[]{:S(2)}) collective-permute-start(bf16[2,16,2048]{2,1,0:T(8,128)(2,1)S(1)} %slice.3), channel_id=1, source_target_pairs={{0,64},{64,128},{128,192},{1,65},{65,129},{129,193},{2,66},{66,130... | collective-permute-start | bytes 393224 | tf_op jit(solution)/shard_map/ppermute | solution.py:236
  3.6 0.6 copy-start

commit v5 on v4

--- a/solution.py
+++ b/solution.py
@@ -87,36 +87,44 @@
 
 
 def channelize_kernel(
-    volts_ref, history_ref, taps_ref, table_ref, out_ref, volts, before, rows, turned, rounded, in_sems, out_sems
+    volts_ref, history_ref, taps_ref, table_ref, out_ref, volts, table, before, rows, turned, rounded, in_sems, out_sems
 ):
     inputs = volts_ref.shape[1]
     taps_count, channels = taps_ref.shape
     block = LANES
     width = block * channels
     reach = taps_count * channels
-    ahead = pltpu.make_async_copy(volts_ref.at[:, :, pl.ds(width - reach, reach)], before, in_sems.at[2, 0])
+    pieces = 4
+    ahead = pltpu.make_async_copy(volts_ref.at[:, :, pl.ds(width - reach, reach)], before, in_sems.at[2, 0, 0])
     ahead.start()
     arriving = {}
     for half in (1, 0):
         for part in range(2):
-            copy = pltpu.make_async_copy(
-                volts_ref.at[part, :, pl.ds(half * width, width)], volts.at[half, part], in_sems.at[half, part]
-            )
-            copy.start()
-            arriving[half, part] = copy
-
-    pieces = 4
+            for n in range(pieces):
+                copy = pltpu.make_async_copy(
+                    volts_ref.at[part, :, pl.ds(half * width + n * (width // pieces), width // pieces)],
+                    volts.at[half, part, :, pl.ds(n * (width // pieces), width // pieces)],
+                    in_sems.at[half, part, n],
+                )
+                copy.start()
+                arriving[half, part, n] = copy
+        if half == 1:
+            tables = pltpu.make_async_copy(table_ref, table, in_sems.at[2, 1, 0])
+            tables.start()
+
     ahead.wait()
-    arriving[1, 0].wait()
     late = filter_steps(volts.at[1], before, taps_ref, rows.at[1], pieces)
     for n in range(2 * channels // LANES * pieces):
-        if n == channels // LANES * pieces:
-            arriving[1, 1].wait()
+        part, tile_piece = divmod(n, channels // LANES * pieces)
+        if tile_piece < pieces:
+            arriving[1, part, tile_piece].wait()
         next(late)
-    arriving[0, 0].wait()
-    arriving[0, 1].wait()
+    for part in range(2):
+        for n in range(pieces):
+            arriving[0, part, n].wait()
+    tables.wait()
     early = filter_steps(volts.at[0], history_ref, taps_ref, rows.at[0], pieces)
-    for _ in dft_steps(table_ref, rows.at[1], turned.at[1], inputs, 2):
+    for _ in dft_steps(table, rows.at[1], turned.at[1], inputs, 2):
         next(early)
         next(early)
     sent = []
@@ -128,7 +136,7 @@
         copy.start()
         sent.append(copy)
 
-    steps = dft_steps(table_ref, rows.at[0], turned.at[0], inputs, 2)
+    steps = dft_steps(table, rows.at[0], turned.at[0], inputs, 2)
     for where in rounding_steps(turned.at[1], rounded.at[1], inputs, inputs // 2):
         send(1, where)
         next(steps)
@@ -146,16 +154,17 @@
     resident = pl.BlockSpec(memory_space=pltpu.VMEM)
     return pl.pallas_call(
         channelize_kernel,
-        in_specs=[pl.BlockSpec(memory_space=pl.ANY), resident, resident, resident],
+        in_specs=[pl.BlockSpec(memory_space=pl.ANY), resident, resident, pl.BlockSpec(memory_space=pl.ANY)],
         out_specs=pl.BlockSpec(memory_space=pl.ANY),
         out_shape=jax.ShapeDtypeStruct((channels, 2, inputs, spectra), jnp.bfloat16),
         scratch_shapes=[
             pltpu.VMEM((2, 2, inputs, block * channels), jnp.bfloat16),
+            pltpu.VMEM((2 * channels, 2 * channels), jnp.bfloat16),
             pltpu.VMEM((2, inputs, taps_count * channels), jnp.bfloat16),
             pltpu.VMEM((2, 2 * channels // LANES, inputs * (block + SPARE), LANES), jnp.float32),
             pltpu.VMEM((2, 2 * channels * (inputs + SPARE), block), jnp.float32),
             pltpu.VMEM((2, channels, 2, inputs, block), jnp.bfloat16),
-            pltpu.SemaphoreType.DMA((3, 2)),
+            pltpu.SemaphoreType.DMA((3, 2, 4)),
             pltpu.SemaphoreType.DMA((inputs // 2 + 4,)),
         ],
         compiler_params=pltpu.CompilerParams(vmem_limit_bytes=VMEM_BYTES),

time: 139 us -> 138 us (level)
  no operation moved by 1% of the time
where the time goes in v5:
time: 138 us
  blocking collectives  116 us (84%)
  Pallas kernels  17.8 us (13%)
  starting transfers between devices  1.75 us (1%)
  local copies, waits for them, and re-layouts  1.55 us (1%)
    all_to_all x1, blocking collectives, per_device(): lax.all_to_all(spectra, ('tm', 'band'), split_axis=0, concat_axis=0, tile...  116 us
    pallas_call x1, Pallas kernels, channelize(): pl.pallas_call(channelize_kernel, in_specs=[pl.BlockSpec(memory_space=pl....  10.6 us
    pallas_call x1, Pallas kernels, correlate(): pl.pallas_call(functools.partial(correlate_kernel, 1.0 / spectra, tile),...  7.27 us
  transfers between devices with their start and end apart: 1, of which 1 were waited for; matrix products, arithmetic and copies ran while one was open for 0% of the time, Pallas kernels for 0%

profile of v5, /device:TPU:6, one launch (start us, length us, event | category | flops | bytes accessed | tf_op | source)
XLA Modules:
  0.0 138.2 jit_solution(12370912965757857061)
XLA Ops:
  0.0 0.9 slice.3
  0.9 1.7 %collective-permute-start = (bf16[2,16,2048]{2,1,0:T(8,128)(2,1)S(1)}, bf16[2,16,2048]{2,1,0:T(8,128)(2,1)S(1)}, u32[]{:S(2)}, u32[]{:S(2)}) collective-permute-start(bf16[2,16,2048]{2,1,0:T(8,128)(2,1)S(1)} %slice.3), channel_id=1, source_target_pairs={{0,64},{64,128},{128,192},{1,65},{65,129},{129,193},{2,66},{66,130... | collective-permute-start | bytes 393224 | tf_op jit(solution)/shard_map/ppermute | solution.py:245
  2.7 1.0 collective-permute-done.history_ref
  3.6 0.0 copy-start
  3.6 0.6 copy-done
  4.3 10.6 %shard_map.37 = bf16[256,2,16,256]{3,2,1,0:T(8,128)(2,1)} custom-call(bf16[2,16,65536]{2,1,0:T(8,128)(2,1)} %volts_ref.1, bf16[2,16,2048]{2,1,0:T(8,128)(2,1)} %copy-done, f32[8,256]{1,0:T(8,128)} %taps_ref.1, bf16[512,512]{1,0:T(8,128)(2,1)} %constant.2.clone.table_ref), custom_call_target="tpu_custom_call" | custom-call | flops 2147483648 | bytes 8388608 | tf_op jit(solution)/shard_map/pallas_call | solution.py:155
  14.9 115.9 %all_to_all.5 = bf16[256,2,16,256]{3,2,1,0:T(8,128)(2,1)S(1)} all-to-all(bf16[256,2,16,256]{3,2,1,0:T(8,128)(2,1)} %shard_map.37), channel_id=1, replica_groups=mesh['tm'=4,'band'=64] {'tm','band'}, dimensions={0} | all-to-all | bytes 8388608 | tf_op jit(solution)/shard_map/all_to_all | solution.py:247
  130.7 7.3 %shard_map.38 = f32[1,2,1024,1024]{3,2,1,0:T(8,128)} custom-call(bf16[4,64,2,16,256]{4,3,2,1,0:T(8,128)(2,1)S(1)} %bitcast.1), custom_call_target="tpu_custom_call" | custom-call | flops 5368709120 | bytes 12582912 | tf_op jit(solution)/shard_map/pallas_call | solution.py:221
Async XLA Ops:
  0.9 2.7 %collective-permute-start = (bf16[2,16,2048]{2,1,0:T(8,128)(2,1)S(1)}, bf16[2,16,2048]{2,1,0:T(8,128)(2,1)S(1)}, u32[]{:S(2)}, u32[]{:S(2)}) collective-permute-start(bf16[2,16,2048]{2,1,0:T(8,128)(2,1)S(1)} %slice.3), channel_id=1, source_target_pairs={{0,64},{64,128},{128,192},{1,65},{65,129},{129,193},{2,66},{66,130... | collective-permute-start | bytes 393224 | tf_op jit(solution)/shard_map/ppermute | solution.py:245
  3.6 0.6 copy-start
